TPU v7x, 32 devices: a whole 2x2x4 slice. The times are simulated.
32 devices in a mesh: group: 2 (over y), col: 8 (over z, x), row: 2 (over core).
Axes of the slice: x: 2, y: 2, z: 4, core: 2. Of those that a mesh axis runs over, the one named last changes fastest.
Arguments:
- tile_values: bfloat16 [768, 256, 256], P(('group', 'col', 'row')), parts along dimension 0, may hold values from -0.75 to 0.75
- tile_blocks: int32 [768, 2], P(('group', 'col', 'row')), parts along dimension 0, may hold values from 0 to 511, as said below
- scale_index: int32 [768], P(('group', 'col', 'row')), parts along dimension 0, may hold values from 0 to 15
- scale_table: float32 [32], P('group'), parts along dimension 0, may hold values from 0.5 to 2
- primal_iter: float32 [16, 16384], P(('group', 'col'), 'row'), parts along dimension 0, may hold values from -6 to 6
- dual_iter: float32 [4, 8192], P(('group', 'row'), 'col'), parts along dimension 0, may hold values from -0.36 to 0.36
- objective: float32 [16, 16384], P(('group', 'col'), 'row'), parts along dimension 0, may hold values from -0.3 to 0.3
- right_side: float32 [4, 8192], P(('group', 'row'), 'col'), parts along dimension 0, may hold values from -6 to 6
- lower_bound: float32 [16, 16384], P(('group', 'col'), 'row'), parts along dimension 0, may hold values from -1.2 to 0.95, as said below
- upper_bound: float32 [16, 16384], P(('group', 'col'), 'row'), parts along dimension 0, may hold values from -0.95 to 1.2, as said below
- bound_kind: int32 [16, 16384], P(('group', 'col'), 'row'), parts along dimension 0, may hold values from 0 to 3
- row_kind: int32 [4, 8192], P(('group', 'row'), 'col'), parts along dimension 0, may hold values from 0 to 1
- step_sizes: float32 [4], P('group'), parts along dimension 0, may hold values from 0.2 to 0.8
Outputs:
- primal_next: float32 [16, 16384], P(('group', 'col'), 'row'), parts along dimension 0
- dual_next: float32 [4, 8192], P(('group', 'row'), 'col'), parts along dimension 0
- restart_stats: float32 [6], P('group'), parts along dimension 0
There are 2 independent parts, one for each index of `group`. A program takes and returns all parts, laid end to end along the dimension named above; each array names one. Nothing has to cross between parts.
Inputs may be any that keep to these rules, and one draw needn't show every extreme that they name: tile_blocks[s, 0] is a row block and tile_blocks[s, 1] a column block. With s a tile's index within its part, g = s // 24, c = g // 2 and r = g % 2, the row block lies in r * 32 to (r + 1) * 32 - 1 and the column block in c * 64 to (c + 1) * 64 - 1. Write o = (row block - r * 32) * 256 // 1024 for the col index whose rows hold a tile's row block: among the 24 tiles of one g, at most 3 share one o, and exactly 3 share some o. lower_bound is below upper_bound in every entry. upper_bound is above lower_bound in every entry.
All inputs are finite; a program needn't handle non-finite values.
Results may differ from a plain program's by a relative error of at most 0.0003.
The roundings to bfloat16 on the way count: a program that leaves them out, or rounds other values in their place, can miss the bound.
Values may be sent and summed in bfloat16 or wider, within the bound.
A program may use at most 64 MiB of HBM per device.

v0:
```python
import math

import jax
import jax.numpy as jnp
from jax import lax
from jax.sharding import PartitionSpec as P


def shards(
    tile_values,
    tile_blocks,
    scale_index,
    scale_table,
    primal_iter,
    dual_iter,
    objective,
    right_side,
    lower_bound,
    upper_bound,
    bound_kind,
    row_kind,
    step_sizes,
):
    tile_size = tile_values.shape[1]
    cols_dev = primal_iter.shape[1]
    rows_dev = dual_iter.shape[1]
    col_count = lax.axis_size("col")
    row_count = lax.axis_size("row")
    cseg_len = cols_dev * row_count
    rseg_len = rows_dev * col_count
    col_span = cseg_len // tile_size
    row_span = rseg_len // tile_size
    col_here = lax.axis_index("col")
    row_here = lax.axis_index("row")
    row_local = tile_blocks[:, 0] - row_here * row_span
    col_local = tile_blocks[:, 1] - col_here * col_span
    table_hit = scale_index[:, None] == jnp.arange(scale_table.shape[0], dtype=jnp.int32)[None, :]
    scales = jnp.sum(jnp.where(table_hit, scale_table[None, :], 0.0), axis=1)
    col_pick = (col_local[:, None] == jnp.arange(col_span, dtype=jnp.int32)[None, :]).astype(
        jnp.float32
    )
    segment = lax.all_gather(dual_iter.astype(jnp.bfloat16), "col", axis=1, tiled=True)
    picked_dual = segment.reshape(row_span, tile_size)[row_local]
    partial_cols = (
        jnp.einsum("stk,st->sk", tile_values, picked_dual, preferred_element_type=jnp.float32)
        * scales[:, None]
    )
    col_terms = jnp.dot(col_pick.T, partial_cols, precision=lax.Precision.HIGHEST).reshape(
        1, cseg_len
    )
    aty = lax.psum_scatter(col_terms, "row", scatter_dimension=1, tiled=True)
    reduced = objective - aty
    has_low = (bound_kind == 1) | (bound_kind == 3)
    has_up = (bound_kind == 2) | (bound_kind == 3)
    moved = primal_iter - step_sizes[0] * reduced
    moved = jnp.where(has_low, jnp.maximum(moved, lower_bound), moved)
    primal_next = jnp.where(has_up, jnp.minimum(moved, upper_bound), moved)
    zero = jnp.zeros_like(reduced)
    dual_resid = jnp.where(
        bound_kind == 0,
        reduced,
        jnp.where(
            bound_kind == 1,
            jnp.minimum(reduced, 0.0),
            jnp.where(bound_kind == 2, jnp.maximum(reduced, 0.0), zero),
        ),
    )
    bound_terms = jnp.where(has_low, lower_bound * jnp.maximum(reduced, 0.0), zero) + jnp.where(
        has_up, upper_bound * jnp.minimum(reduced, 0.0), zero
    )
    dual_block_share = jnp.sum(dual_resid * dual_resid)
    gap_local = (
        jnp.sum(objective * primal_next) - jnp.sum(right_side * dual_iter) - jnp.sum(bound_terms)
    )
    dual_sum, gap_sum = lax.psum((dual_block_share, gap_local), ("col", "row"))
    stacked = jnp.concatenate([2.0 * primal_next - primal_iter, primal_next], axis=0).astype(
        jnp.bfloat16
    )
    gathered = lax.all_gather(stacked, "row", axis=1, tiled=True)
    picked_primal = gathered.reshape(2, col_span, tile_size)[:, col_local]
    products = (
        jnp.einsum("stk,vsk->svt", tile_values, picked_primal, preferred_element_type=jnp.float32)
        * scales[:, None, None]
    )
    row_pick = (row_local[:, None] == jnp.arange(row_span, dtype=jnp.int32)[None, :]).astype(
        jnp.float32
    )
    row_terms = jnp.einsum(
        "sr,svt->vrt", row_pick, products, precision=lax.Precision.HIGHEST
    ).reshape(2, rseg_len)
    totals = lax.psum(row_terms, "col")
    own_rows = lax.dynamic_slice_in_dim(totals, col_here * rows_dev, rows_dev, 1)
    ineq = row_kind == 1
    dual_next = dual_iter + step_sizes[1] * (right_side - own_rows[0:1])
    dual_next = jnp.where(ineq, jnp.maximum(dual_next, 0.0), dual_next)
    primal_resid = right_side - own_rows[1:2]
    primal_resid = jnp.where(ineq, jnp.maximum(primal_resid, 0.0), primal_resid)
    primal_local = jnp.sum(primal_resid * primal_resid)
    primal_sum = lax.psum(primal_local, ("col", "row"))
    rows_total = rseg_len * row_count
    cols_total = cseg_len * col_count
    restart_stats = jnp.stack(
        [primal_sum / rows_total, dual_sum / cols_total, gap_sum / math.sqrt(cols_total)]
    )
    return (primal_next, dual_next, restart_stats)


def solution(mesh):
    return jax.shard_map(
        shards,
        mesh=mesh,
        in_specs=(
            P(("group", "col", "row"), None, None),
            P(("group", "col", "row"), None),
            P(("group", "col", "row")),
            P("group"),
            P(("group", "col"), "row"),
            P(("group", "row"), "col"),
            P(("group", "col"), "row"),
            P(("group", "row"), "col"),
            P(("group", "col"), "row"),
            P(("group", "col"), "row"),
            P(("group", "col"), "row"),
            P(("group", "row"), "col"),
            P("group"),
        ),
        out_specs=(P(("group", "col"), "row"), P(("group", "row"), "col"), P("group")),
        check_vma=False,
    )
```

profile of v0, /device:TPU:0, one launch (start us, length us, event | category | flops | bytes accessed | tf_op | source)
XLA Modules:
  0.0 195.2 jit_solution(15565132101926710492)
XLA Ops:
  7.3 0.9 fusion.17
  8.1 0.8 convert_element_type.2
  8.9 32.2 %all_gather.6 = bf16[1,8192]{1,0:T(2,128)(2,1)S(1)} all-gather(bf16[1,1024]{1,0:T(2,128)(2,1)S(1)} %convert_element_type.2), channel_id=1, replica_groups=mesh['group'=2,'col'=8,'row'=2] {'col'}, dimensions={1}, use_global_device_ids=true | all-gather | bytes 18432 | tf_op jit(solution)/shard_map/all_gather | solution.py:42
  41.1 0.1 reduce
  41.2 0.6 gather_fusion
  41.8 0.5 fusion.3
  42.3 0.1 select_reduce_fusion
  42.4 0.3 convolution_bitcast_fusion.1
  42.8 4.9 %copy.23 = f32[1,16384]{0,1:T(8,128)} copy(f32[1,16384]{1,0:T(1,128)S(1)} %bitcast.41) | data formatting | bytes 131072
  47.7 5.7 %bitcast_bitcast_fusion = f32[16384,1]{1,0:T(8,128)} fusion(f32[1,16384]{0,1:T(8,128)} %copy.23), kind=kLoop, calls=%fused_computation.2 | loop fusion | bytes 131072
  53.5 0.5 copy-done.10
  54.1 0.6 fusion.18
  54.6 16.7 %reduce-scatter.4.cloned.1.call-done = f32[8192,1]{1,0:T(8,128)} async-done(((f32[16384,1]{1,0:T(8,128)}), f32[8192,1]{1,0:T(8,128)}) %reduce-scatter.4.cloned.1.call-update) | async-done | bytes 32784
  71.3 2.8 %copy.21 = f32[1,8192]{1,0:T(1,128)S(1)} copy(f32[1,8192]{0,1:T(8,128)} %bitcast.40) | data formatting | bytes 65536
  74.2 1.8 multiply_reduce_fusion.1
  76.1 1.9 all_gather.7
  78.0 0.6 gather_fusion.1
  78.6 0.9 convolution_multiply_fusion
  79.5 0.3 convolution_bitcast_fusion
  79.8 0.7 copy.24
  80.5 69.9 %all-reduce.3.cloned.1.call-done = f32[2,8192]{1,0:T(2,128)} async-done(((f32[2,8192]{1,0:T(2,128)}), f32[2,8192]{1,0:T(2,128)}) %all-reduce.3.cloned.1.call-update) | async-done | bytes 65552 | tf_op jit(solution)/shard_map/psum | solution.py:91
  150.4 2.7 %fusion.13 = (f32[]{:T(128)}, f32[]{:T(128)}, f32[1,1024]{1,0:T(1,128)}) fusion(f32[1,1024]{1,0:T(1,128)S(1)} %copy-done.8, f32[2,8192]{1,0:T(2,128)} %all-reduce.3.cloned.1.call-done, s32[]{:T(128)S(6)} %add.33, s32[]{:T(128)S(6)} %select_n.49, s32[1,1024]{1,0:T(1,128)S(1)} %copy-done.9, f32[1,1024]{1,0:T(1,128)S(1)} %copy-done.7, f32[]{:T(128)} %bitcast.5), kind=kLoop, calls=%fused_computation.42 | loop fusion | flops 13310 | bytes 24596 | tf_op jit(solution)/shard_map/reduce_sum | solution.py:98
  155.0 31.0 %all-reduce = (f32[]{:T(128)}, f32[]{:T(128)}, f32[]{:T(128)}) all-reduce(f32[]{:T(128)S(6)} %sub.47, f32[]{:T(128)} %get-tuple-element.3, f32[]{:T(128)} %get-tuple-element.6), channel_id=1, replica_groups=mesh['group'=2,'col'=8,'row'=2] {'col','row'}, use_global_device_ids=true, to_apply=%region_10.11 | all-reduce | flops 3 | bytes 24 | tf_op jit(solution)/shard_map/psum | solution.py:75
  187.8 0.6 pad_maximum_fusion.1
  (35 shorter events, 0.4 us)
Async XLA Ops:
  7.2 34.6 %copy-start = (bf16[24,256,256]{2,1,0:T(8,128)(2,1)S(1)}, bf16[24,256,256]{2,1,0:T(8,128)(2,1)}, u32[]{:S(2)}) copy-start(bf16[24,256,256]{2,1,0:T(8,128)(2,1)} %param.13) | copy-start | bytes 9437188
  7.2 35.1 %copy-start.12 = (s32[24]{0:T(128)S(1)}, s32[24]{0:T(128)}, u32[]{:S(2)}) copy-start(s32[24]{0:T(128)} %param.15) | copy-start | bytes 292
  7.2 35.1 %copy-start.11 = (f32[16]{0:T(128)S(1)}, f32[16]{0:T(128)}, u32[]{:S(2)}) copy-start(f32[16]{0:T(128)} %param.16) | copy-start | bytes 196
  7.2 64.1 %reduce-scatter.4.cloned.1.call-start = ((), (), s32[]{:S(2)}) async-start(), calls=%async_computation.2 | async-start | bytes 12582912
  53.4 0.7 copy-start.10
  53.4 20.7 %copy-start.1 = (f32[1,8192]{1,0:T(1,128)S(1)}, f32[1,8192]{1,0:T(1,128)}, u32[]{:S(2)}) copy-start(f32[1,8192]{1,0:T(1,128)} %param.17) | copy-start | bytes 98308
  53.4 20.7 %copy-start.3 = (s32[1,8192]{1,0:T(1,128)S(1)}, s32[1,8192]{1,0:T(1,128)}, u32[]{:S(2)}) copy-start(s32[1,8192]{1,0:T(1,128)} %param.23) | copy-start | bytes 98308
  53.4 20.7 %copy-start.4 = (f32[1,8192]{1,0:T(1,128)S(1)}, f32[1,8192]{1,0:T(1,128)}, u32[]{:S(2)}) copy-start(f32[1,8192]{1,0:T(1,128)} %param.19) | copy-start | bytes 98308
  53.5 20.7 %copy-start.5 = (f32[1,8192]{1,0:T(1,128)S(1)}, f32[1,8192]{1,0:T(1,128)}, u32[]{:S(2)}) copy-start(f32[1,8192]{1,0:T(1,128)} %param.22) | copy-start | bytes 98308
  53.5 20.7 %copy-start.6 = (f32[1,8192]{1,0:T(1,128)S(1)}, f32[1,8192]{1,0:T(1,128)}, u32[]{:S(2)}) copy-start(f32[1,8192]{1,0:T(1,128)} %param.21) | copy-start | bytes 98308
  53.5 96.9 %all-reduce.3.cloned.1.call-start = ((), (), s32[]{:S(2)}) async-start(), calls=%async_computation.1 | async-start | bytes 131072 | tf_op jit(solution)/shard_map/psum | solution.py:91
  74.1 76.3 %copy-start.7 = (f32[1,1024]{1,0:T(1,128)S(1)}, f32[1,1024]{1,0:T(1,128)}, u32[]{:S(2)}) copy-start(f32[1,1024]{1,0:T(1,128)} %param.18) | copy-start | bytes 12292
  74.1 76.3 %copy-start.8 = (f32[1,1024]{1,0:T(1,128)S(1)}, f32[1,1024]{1,0:T(1,128)}, u32[]{:S(2)}) copy-start(f32[1,1024]{1,0:T(1,128)} %param.20) | copy-start | bytes 12292
  74.1 76.3 %copy-start.9 = (s32[1,1024]{1,0:T(1,128)S(1)}, s32[1,1024]{1,0:T(1,128)}, u32[]{:S(2)}) copy-start(s32[1,1024]{1,0:T(1,128)} %param.24) | copy-start | bytes 12292
  76.0 112.4 %copy-start.2 = (f32[1,8192]{1,0:T(1,128)}, f32[1,8192]{1,0:T(1,128)S(1)}, u32[]{:S(2)}) copy-start(f32[1,8192]{1,0:T(1,128)S(1)} %get-tuple-element.11) | copy-start | bytes 98308
Sparse Core Ops, SparseCore 0:
  53.5 17.6 reduce-scatter.3
  80.6 69.7 all-reduce.2
where the time goes:
time: 196 us; the launch traced here: 195 us
  waiting for transfers between devices  86.6 us (44%)
  blocking collectives  65 us (33%)
  between operations  18 us (9%)
  local copies, waits for them, and re-layouts  16.6 us (8%)
  other arithmetic  6.95 us (4%)
  matrix products  2.03 us (1%)
    psum x1, waiting for transfers between devices, shards(): totals = lax.psum(row_terms, 'col')  69.9 us
    all_gather x1, blocking collectives, shards(): lax.all_gather(dual_iter.astype(jnp.bfloat16), 'col', axis=1, tiled=True)  32.2 us
    psum x1, blocking collectives, shards(): dual_sum, gap_sum = lax.psum((dual_block_share, gap_local), ('col', 'row'))  31 us
    unnamed x3, waiting for transfers between devices  16.7 us
    unnamed x31, local copies, waits for them, and re-layouts  14.8 us
  transfers between devices with their start and end apart: 2, of which 2 were waited for; matrix products, arithmetic and copies ran while one was open for 0% of the time, Pallas kernels for 0%

commit v1 on v0

v1 whole, which is shorter than its diff:
```python
import functools
import math

import jax
import jax.numpy as jnp
from jax import lax
from jax.experimental import pallas as pl
from jax.experimental.pallas import tpu as pltpu
from jax.sharding import PartitionSpec as P

F32 = jnp.float32
BF16 = jnp.bfloat16
MESH = pl.DeviceIdType.MESH
LANES = 128


def each(count, body):
    if count <= 17:
        for k in range(1, count):
            body(k)
    else:
        lax.fori_loop(1, count, lambda k, _: (body(k), 0)[1], 0)


def three_parts(v):
    hi = v.astype(BF16)
    rest = v - hi.astype(F32)
    mid = rest.astype(BF16)
    low = (rest - mid.astype(F32)).astype(BF16)
    return hi, mid, low


def iota(shape, dim):
    return lax.broadcasted_iota(jnp.int32, shape, dim)


def kernel(
    n_col,
    n_row,
    tv, tb, si, st, x_h, y_h, c_h, b_h, l_h, u_h, k_h, e_h, step,
    xn_o, yn_o, stat_o,
    tiles, prim, kind, ybuf, bbuf, ebuf, meta, part, xn_s, yn_s, terms, rt, sbuf,
    lsem, ysend, yrecv, rsend, rrecv, tsend, trecv, ssend, srecv,
):
    count, size, _ = tv.shape
    groups = count // 8
    cblocks = prim.shape[2]
    n_dev = n_col * n_row
    col = lax.axis_index("col")
    row = lax.axis_index("row")
    other = 1 - row
    dev = col * n_row + row
    row_span = ybuf.shape[1] // 2 * n_col
    col_span = cblocks

    y_in = pltpu.make_async_copy(y_h, ybuf.at[col], lsem.at[0])
    y_in.start()

    barrier = pltpu.get_barrier_semaphore()

    def greet(k):
        q = lax.rem(dev + k, n_dev)
        pl.semaphore_signal(
            barrier,
            inc=1,
            device_id={"col": lax.div(q, n_row), "row": lax.rem(q, n_row)},
            device_id_type=MESH,
        )

    each(n_dev, greet)

    chunk = count // 4
    tile_in = []
    for i in range(4):
        span = pl.ds(i * chunk, chunk)
        copy = pltpu.make_async_copy(tv.at[span], tiles.at[span], lsem.at[1 + i])
        copy.start()
        tile_in.append(copy)
    small_in = [
        pltpu.make_async_copy(src, prim.at[i, row], lsem.at[5 + i])
        for i, src in enumerate((x_h, c_h, l_h, u_h))
    ]
    small_in.append(pltpu.make_async_copy(k_h, kind.at[row], lsem.at[9]))
    small_in.append(pltpu.make_async_copy(b_h, bbuf, lsem.at[10]))
    small_in.append(pltpu.make_async_copy(e_h, ebuf, lsem.at[11]))
    for copy in small_in:
        copy.start()

    sub8 = iota((8, LANES), 0)
    lane8 = iota((8, LANES), 1)
    lane256 = iota((8, 2 * LANES), 1)
    rows_l = [tb[0, s] - row * row_span for s in range(count)]
    cols_l = [tb[1, s] - col * col_span for s in range(count)]
    own = lane8 // 64 == row
    spot = lane8 % 64
    mine = jnp.where(own, -1.0, 0.0)
    for s in range(count):
        at = (2 * cols_l[s]).astype(F32)
        mine = jnp.where(own & (spot == s), at, mine)
        mine = jnp.where(own & (spot == 32 + s), at + 1.0, mine)
    meta[row] = mine

    y_in.wait()
    pl.semaphore_wait(barrier, n_dev - 1)

    def y_copy(at, to, sem):
        return pltpu.make_async_remote_copy(
            src_ref=ybuf.at[col],
            dst_ref=ybuf.at[at],
            send_sem=ysend.at[sem],
            recv_sem=yrecv.at[at],
            device_id={"col": to},
            device_id_type=MESH,
        )

    each(n_col, lambda k: y_copy(col, lax.rem(col + k, n_col), k).start())

    def row_copy(src, dst, i):
        return pltpu.make_async_remote_copy(
            src_ref=src,
            dst_ref=dst,
            send_sem=rsend.at[i],
            recv_sem=rrecv.at[i],
            device_id={"row": other},
            device_id_type=MESH,
        )

    early = [row_copy(src, prim.at[i, row], i) for i, src in enumerate((x_h, c_h, l_h, u_h))]
    early.append(row_copy(k_h, kind.at[row], 4))
    early.append(row_copy(meta.at[row], meta.at[row], 5))
    for copy in early:
        copy.start()

    scales = [st[si[s]] for s in range(count)]
    scale8, row8, col8 = [], [], []
    for g in range(groups):
        sc = jnp.zeros((8, LANES), F32)
        rr = jnp.zeros((8, LANES), jnp.int32)
        cc = jnp.zeros((8, LANES), jnp.int32)
        for t in range(8):
            s = g * 8 + t
            sc = jnp.where(sub8 == t, scales[s], sc)
            rr = jnp.where(sub8 == t, 2 * rows_l[s], rr)
            cc = jnp.where(sub8 == t, 2 * cols_l[s], cc)
        scale8.append(jnp.concatenate([sc, sc], axis=1))
        row8.append(rr)
        col8.append(cc)

    wide_rows = ybuf.shape[1] * n_col
    tgt_y = jnp.concatenate(row8 + [jnp.full((8, LANES), -2, jnp.int32)], axis=0)
    reps = max(1, wide_rows // LANES)
    if wide_rows < LANES:
        tgt_y = tgt_y[:, :wide_rows]
    else:
        tgt_y = jnp.concatenate([tgt_y] * reps, axis=1)
    lane_y = iota(tgt_y.shape, 1)
    pick_y = [(lane_y == tgt_y + h).astype(F32).astype(BF16) for h in range(2)]

    tgt_p = jnp.concatenate([v for cc in col8 for v in (cc, cc + 2 * col_span)], axis=0)
    reps = 4 * col_span // LANES
    tgt_p = jnp.concatenate([tgt_p] * reps, axis=1)
    lane_p = iota(tgt_p.shape, 1)
    pick_p = [(lane_p == tgt_p + h).astype(F32).astype(BF16) for h in range(2)]

    spot3 = lane256 % (2 * count)
    live = lane256 < 6 * count
    tgt_r = jnp.full((8, 2 * LANES), -1, jnp.int32)
    for s in range(count):
        tgt_r = jnp.where(live & (spot3 == s), 2 * rows_l[s], tgt_r)
        tgt_r = jnp.where(live & (spot3 == count + s), 2 * rows_l[s] + 1, tgt_r)
    place_r = (iota((wide_rows, 2 * LANES), 0) == tgt_r[0:1]).astype(F32).astype(BF16)

    for copy in tile_in:
        copy.wait()
    each(n_col, lambda k: y_copy(lax.rem(col + k, n_col), col, k).wait_recv())

    y_b = ybuf[...].reshape(wide_rows, LANES).astype(BF16)
    y_pick = jnp.concatenate(
        [jnp.dot(pick, y_b, preferred_element_type=F32) for pick in pick_y], axis=1
    )
    sub_y = iota(y_pick.shape, 0)
    lhs = jnp.concatenate(
        [jnp.where(sub_y == s, y_pick, 0.0).astype(BF16) for s in range(count)], axis=1
    )
    product = jnp.dot(lhs, tiles[...].reshape(count * size, size), preferred_element_type=F32)
    product = product * jnp.concatenate(scale8 + [jnp.zeros((8, 2 * LANES), F32)], axis=0)
    part[row, 0] = product[:, :LANES]
    part[row, 1] = product[:, LANES:]
    part_copy = row_copy(part.at[row], part.at[row], 6)
    part_copy.start()

    for copy in small_in:
        copy.wait()
    late = [row_copy(x_h, prim.at[i, other], i) for i in range(4)]
    late.append(row_copy(k_h, kind.at[other], 4))
    late.append(row_copy(meta.at[row], meta.at[other], 5))
    for copy in late:
        copy.wait_recv()
    targets = (meta[0] + meta[1])[0:1]
    place_c = (iota((2 * col_span, LANES), 0).astype(F32) == targets).astype(F32).astype(BF16)
    place_c = jnp.concatenate([place_c] * 3, axis=1)

    row_copy(part.at[row], part.at[other], 6).wait_recv()
    pieces = jnp.concatenate(three_parts(part[...].reshape(LANES, LANES)), axis=0)
    aty = jnp.dot(place_c, pieces, preferred_element_type=F32)

    full = (2 * cblocks, LANES)
    x, c, low, high = [prim[i].reshape(full) for i in range(4)]
    kinds = kind[...].reshape(full)
    reduced = c - aty
    has_low = (kinds == 1) | (kinds == 3)
    has_up = (kinds == 2) | (kinds == 3)
    moved = x - step[0] * reduced
    moved = jnp.where(has_low, jnp.maximum(moved, low), moved)
    x_next = jnp.where(has_up, jnp.minimum(moved, high), moved)
    xn_s[...] = x_next.reshape(xn_s.shape)
    pair = jnp.concatenate([2.0 * x_next - x, x_next], axis=0).astype(BF16)

    p_pick = jnp.concatenate(
        [jnp.dot(pick, pair, preferred_element_type=F32) for pick in pick_p], axis=1
    )
    sub16 = iota((16, size), 0) % 8
    bars, news = [], []
    for g in range(groups):
        rows16 = p_pick[16 * g : 16 * g + 16]
        acc = jnp.zeros((16, size), F32)
        for t in range(8):
            acc = acc + lax.dot_general(
                jnp.where(sub16 == t, rows16, 0.0).astype(BF16),
                tiles[8 * g + t],
                (((1,), (1,)), ((), ())),
                preferred_element_type=F32,
            )
        bars.append(acc[:8] * scale8[g])
        news.append(acc[8:] * scale8[g])
    bar = jnp.concatenate(bars, axis=0)
    new = jnp.concatenate(news, axis=0)
    stacked = jnp.concatenate(
        [
            jnp.concatenate([bar[:, :LANES], new[:, :LANES]], axis=1),
            jnp.concatenate([bar[:, LANES:], new[:, LANES:]], axis=1),
        ],
        axis=0,
    )
    pad = jnp.zeros((2 * LANES - 6 * count, 2 * LANES), BF16)
    pieces = jnp.concatenate(three_parts(stacked) + (pad,), axis=0)
    terms[...] = jnp.dot(place_r, pieces, preferred_element_type=F32).reshape(terms.shape)

    def t_copy(src, at, to, sem):
        return pltpu.make_async_remote_copy(
            src_ref=terms.at[src],
            dst_ref=rt.at[at],
            send_sem=tsend.at[sem],
            recv_sem=trecv.at[at],
            device_id={"col": to},
            device_id_type=MESH,
        )

    def t_start(k):
        to = lax.rem(col + k, n_col)
        t_copy(to, col, to, k).start()

    each(n_col, t_start)
    rt[col] = terms[col]

    xn_out = pltpu.make_async_copy(xn_s.at[row], xn_o, lsem.at[12])
    xn_out.start()
    resid = jnp.where(
        kinds == 0,
        reduced,
        jnp.where(
            kinds == 1,
            jnp.minimum(reduced, 0.0),
            jnp.where(kinds == 2, jnp.maximum(reduced, 0.0), 0.0),
        ),
    )
    bounds = jnp.where(has_low, low * jnp.maximum(reduced, 0.0), 0.0) + jnp.where(
        has_up, high * jnp.minimum(reduced, 0.0), 0.0
    )
    y = ybuf[col]
    b = bbuf[...]
    dual_sum = 0.5 * jnp.sum(resid * resid, axis=0, keepdims=True)
    gap = 0.5 * jnp.sum(c * x_next - bounds, axis=0, keepdims=True) - jnp.sum(
        b * y, axis=0, keepdims=True
    )
    ineq = ebuf[...] == 1

    def t_wait(k):
        t_copy(0, lax.rem(col + k, n_col), col, k).wait_recv()

    each(n_col, t_wait)
    totals = jnp.sum(rt[...], axis=0)
    y_next = y + step[1] * (b - totals[:, :LANES])
    yn_s[...] = jnp.where(ineq, jnp.maximum(y_next, 0.0), y_next)
    p_resid = b - totals[:, LANES:]
    p_resid = jnp.where(ineq, jnp.maximum(p_resid, 0.0), p_resid)
    primal_sum = jnp.sum(p_resid * p_resid, axis=0, keepdims=True)
    sbuf[dev] = jnp.where(
        sub8 == 0, primal_sum, jnp.where(sub8 == 1, dual_sum, jnp.where(sub8 == 2, gap, 0.0))
    )

    def s_copy(at, to, sem):
        return pltpu.make_async_remote_copy(
            src_ref=sbuf.at[dev],
            dst_ref=sbuf.at[at],
            send_sem=ssend.at[sem],
            recv_sem=srecv.at[at],
            device_id={"col": lax.div(to, n_row), "row": lax.rem(to, n_row)},
            device_id_type=MESH,
        )

    each(n_dev, lambda k: s_copy(dev, lax.rem(dev + k, n_dev), k).start())
    yn_out = pltpu.make_async_copy(yn_s, yn_o, lsem.at[13])
    yn_out.start()
    for copy in early:
        copy.wait_send()
    part_copy.wait_send()
    each(n_col, lambda k: y_copy(col, col, k).wait_send())
    each(n_col, lambda k: t_copy(0, col, col, k).wait_send())
    xn_out.wait()
    yn_out.wait()

    each(n_dev, lambda k: s_copy(lax.rem(dev + k, n_dev), dev, k).wait_recv())
    sums = jnp.sum(jnp.sum(sbuf[...], axis=0), axis=1, keepdims=True)
    rows_total = ybuf.shape[1] * LANES * n_dev
    cols_total = cblocks * LANES * n_dev
    lane1 = iota((1, LANES), 1)
    stat_o[...] = jnp.where(
        lane1 == 0,
        sums[0:1] / rows_total,
        jnp.where(lane1 == 1, sums[1:2] / cols_total, sums[2:3] / math.sqrt(cols_total)),
    )
    each(n_dev, lambda k: s_copy(dev, dev, k).wait_send())


def shards(
    tile_values,
    tile_blocks,
    scale_index,
    scale_table,
    primal_iter,
    dual_iter,
    objective,
    right_side,
    lower_bound,
    upper_bound,
    bound_kind,
    row_kind,
    step_sizes,
):
    n_col = lax.axis_size("col")
    n_row = lax.axis_size("row")
    n_dev = n_col * n_row
    count, size, _ = tile_values.shape
    cb = primal_iter.shape[1] // LANES
    rb = dual_iter.shape[1] // LANES
    wide = lambda a: a.reshape(-1, LANES)
    hbm = pl.BlockSpec(memory_space=pltpu.HBM)
    smem = pl.BlockSpec(memory_space=pltpu.SMEM)
    vmem = pl.BlockSpec(memory_space=pltpu.VMEM)
    dma = pltpu.SemaphoreType.DMA
    x_next, y_next, stats = pl.pallas_call(
        functools.partial(kernel, n_col, n_row),
        out_shape=(
            jax.ShapeDtypeStruct((cb, LANES), F32),
            jax.ShapeDtypeStruct((rb, LANES), F32),
            jax.ShapeDtypeStruct((1, LANES), F32),
        ),
        in_specs=[hbm, smem, smem, smem, hbm, hbm, hbm, hbm, hbm, hbm, hbm, hbm, smem],
        out_specs=(hbm, hbm, vmem),
        scratch_shapes=[
            pltpu.VMEM((count, size, size), BF16),
            pltpu.VMEM((4, n_row, cb, LANES), F32),
            pltpu.VMEM((n_row, cb, LANES), jnp.int32),
            pltpu.VMEM((n_col, rb, LANES), F32),
            pltpu.VMEM((rb, LANES), F32),
            pltpu.VMEM((rb, LANES), jnp.int32),
            pltpu.VMEM((n_row, 8, LANES), F32),
            pltpu.VMEM((n_row, 2, 32, LANES), F32),
            pltpu.VMEM((n_row, cb, LANES), F32),
            pltpu.VMEM((rb, LANES), F32),
            pltpu.VMEM((n_col, rb, 2 * LANES), F32),
            pltpu.VMEM((n_col, rb, 2 * LANES), F32),
            pltpu.VMEM((n_dev, 8, LANES), F32),
            dma((14,)),
            dma((n_col,)),
            dma((n_col,)),
            dma((7,)),
            dma((7,)),
            dma((n_col,)),
            dma((n_col,)),
            dma((n_dev,)),
            dma((n_dev,)),
        ],
        compiler_params=pltpu.CompilerParams(
            collective_id=0, has_side_effects=True, vmem_limit_bytes=64 * 1024 * 1024
        ),
    )(
        tile_values,
        tile_blocks.T,
        scale_index,
        scale_table,
        wide(primal_iter),
        wide(dual_iter),
        wide(objective),
        wide(right_side),
        wide(lower_bound),
        wide(upper_bound),
        wide(bound_kind),
        wide(row_kind),
        step_sizes,
    )
    return (x_next.reshape(1, -1), y_next.reshape(1, -1), stats[0, :3])


def solution(mesh):
    return jax.shard_map(
        shards,
        mesh=mesh,
        in_specs=(
            P(("group", "col", "row"), None, None),
            P(("group", "col", "row"), None),
            P(("group", "col", "row")),
            P("group"),
            P(("group", "col"), "row"),
            P(("group", "row"), "col"),
            P(("group", "col"), "row"),
            P(("group", "row"), "col"),
            P(("group", "col"), "row"),
            P(("group", "col"), "row"),
            P(("group", "col"), "row"),
            P(("group", "row"), "col"),
            P("group"),
        ),
        out_specs=(P(("group", "col"), "row"), P(("group", "row"), "col"), P("group")),
        check_vma=False,
    )
```

time: 196 us -> 27.1 us (0.14)
  waiting for transfers between devices: 86.6 us -> 0 us
  blocking collectives: 65 us -> 0 us
  Pallas kernels: 0 us -> 22.5 us
  between operations: 18 us -> 0.64 us
  local copies, waits for them, and re-layouts: 16.6 us -> 3.79 us
  other arithmetic: 6.95 us -> 0 us
  matrix products: 2.03 us -> 0 us
    psum x1 -> x0, waiting for transfers between devices: 69.9 us -> none  [shards(): totals = lax.psum(row_terms, 'col')]
    all_gather x2 -> x0, blocking collectives: 34 us -> none  [the longest x1 32.2 us: shards(): lax.all_gather(dual_iter.astype(jnp.bfloat16), 'col', axis=1, tiled=True)]
    psum x1 -> x0, blocking collectives: 31 us -> none  [shards(): dual_sum, gap_sum = lax.psum((dual_block_share, gap_local), ('col', 'row'))]
    pallas_call x0 -> x1, Pallas kernels: none -> 22.5 us  [shards(): pl.pallas_call(functools.partial(kernel, n_col, n_row), out_shape=(jax.Sh...]
    unnamed x3 -> x0, waiting for transfers between devices: 16.7 us -> none
    unnamed x31 -> x2, local copies, waits for them, and re-layouts: 14.8 us -> 2.65 us
    reduce_sum x3 -> x0, other arithmetic: 4.52 us -> none  [the longest x1 2.66 us: shards(): primal_local = jnp.sum(primal_resid * primal_resid)]
    dot_general x4 -> x0, matrix products: 2.03 us -> none  [the longest x1 0.91 us: shards(): jnp.einsum('stk,vsk->svt', tile_values, picked_primal, preferred_element_...]
  transfers between devices with their start and end apart: 2 -> 0, of which waited for: 2 -> 0; matrix products, arithmetic and copies ran while one was open for 0% -> 0% of each run, Pallas kernels for 0% -> 0%
where the time goes in v1:
time: 27.1 us; the launch traced here: 26.9 us
  Pallas kernels  22.5 us (83%)
  local copies, waits for them, and re-layouts  3.79 us (14%)
  between operations  0.64 us (2%)
    pallas_call x1, Pallas kernels, shards(): pl.pallas_call(functools.partial(kernel, n_col, n_row), out_shape=(jax.Sh...  22.5 us
    unnamed x2, local copies, waits for them, and re-layouts  2.65 us
    squeeze x1, local copies, waits for them, and re-layouts, shards(): return (x_next.reshape(1, -1), y_next.reshape(1, -1), stats[0, :3])  1.15 us

profile of v1, /device:TPU:0, one launch (start us, length us, event | category | flops | bytes accessed | tf_op | source)
XLA Modules:
  0.0 26.9 jit_solution(6135341341709270984)
XLA Ops:
  0.6 22.5 %shard_map.148 = (f32[64,128]{1,0:T(8,128)}, f32[8,128]{1,0:T(8,128)}, f32[1,128]{1,0:T(1,128)}) custom-call(bf16[24,256,256]{2,1,0:T(8,128)(2,1)} %tv.1, s32[2,24]{1,0:T(2,128)} %bitcast.23, s32[24]{0:T(128)} %si.1, f32[16]{0:T(128)} %st.1, f32[64,128]{1,0:T(8,128)} %bitcast.13, f32[8,128]{1,0:T(8,128)} %bitcast.19, f32[64,128]{1,0:T(8,128)} %bitcast.14, ...), custom_call_target="tpu_custom_call" | custom-call | tf_op jit(solution)/shard_map/pallas_call | solution.py:362
  23.1 1.1 %slice_bitcast_fusion = f32[3]{0:T(128)} fusion(f32[1,128]{1,0:T(1,128)} %get-tuple-element.8), kind=kLoop, calls=%fused_computation | loop fusion | bytes 24 | tf_op jit(solution)/shard_map/squeeze | solution.py:413
  24.2 1.4 %copy.18 = f32[1,8192]{1,0:T(1,128)} copy(f32[1,8192]{1,0:T(1,128)} %bitcast.18) | data formatting | bytes 65536
  25.6 1.3 %copy.19 = f32[1,1024]{1,0:T(1,128)} copy(f32[1,1024]{1,0:T(1,128)} %bitcast.22) | data formatting | bytes 8192

commit v2 on v1

--- a/solution.py
+++ b/solution.py
@@ -30,6 +30,10 @@
     return hi, mid, low
 
 
+def total(v):
+    return jnp.sum(jnp.sum(v, axis=0, keepdims=True), axis=1, keepdims=True)
+
+
 def iota(shape, dim):
     return lax.broadcasted_iota(jnp.int32, shape, dim)
 
@@ -37,10 +41,10 @@
 def kernel(
     n_col,
     n_row,
-    tv, tb, si, st, x_h, y_h, c_h, b_h, l_h, u_h, k_h, e_h, step,
+    tv, tb_h, si_h, st_h, x_h, y_h, c_h, b_h, l_h, u_h, k_h, e_h, step_h,
     xn_o, yn_o, stat_o,
     tiles, prim, kind, ybuf, bbuf, ebuf, meta, part, xn_s, yn_s, terms, rt, sbuf,
-    lsem, ysend, yrecv, rsend, rrecv, tsend, trecv, ssend, srecv,
+    tb, si, st, step, lsem, ysend, yrecv, rsend, rrecv, tsend, trecv, ssend, srecv,
 ):
     count, size, _ = tv.shape
     groups = count // 8
@@ -53,9 +57,6 @@
     row_span = ybuf.shape[1] // 2 * n_col
     col_span = cblocks
 
-    y_in = pltpu.make_async_copy(y_h, ybuf.at[col], lsem.at[0])
-    y_in.start()
-
     barrier = pltpu.get_barrier_semaphore()
 
     def greet(k):
@@ -69,6 +70,14 @@
 
     each(n_dev, greet)
 
+    y_in = pltpu.make_async_copy(y_h, ybuf.at[col], lsem.at[0])
+    y_in.start()
+    scalar_in = [
+        pltpu.make_async_copy(src, dst, lsem.at[14 + i])
+        for i, (src, dst) in enumerate(((tb_h, tb), (si_h, si), (st_h, st), (step_h, step)))
+    ]
+    for copy in scalar_in:
+        copy.start()
     chunk = count // 4
     tile_in = []
     for i in range(4):
@@ -86,6 +95,8 @@
     for copy in small_in:
         copy.start()
 
+    for copy in scalar_in:
+        copy.wait()
     sub8 = iota((8, LANES), 0)
     lane8 = iota((8, LANES), 1)
     lane256 = iota((8, 2 * LANES), 1)
@@ -279,9 +290,13 @@
     )
     y = ybuf[col]
     b = bbuf[...]
-    dual_sum = 0.5 * jnp.sum(resid * resid, axis=0, keepdims=True)
-    gap = 0.5 * jnp.sum(c * x_next - bounds, axis=0, keepdims=True) - jnp.sum(
-        b * y, axis=0, keepdims=True
+    dual_sum = 0.5 * total(resid * resid)
+    gap = 0.5 * total(c * x_next - bounds) - total(b * y)
+    lane1 = iota((1, LANES), 1)
+    rows_total = ybuf.shape[1] * LANES * n_dev
+    cols_total = cblocks * LANES * n_dev
+    early_stats = jnp.where(
+        lane1 == 1, dual_sum / cols_total, jnp.where(lane1 == 2, gap / math.sqrt(cols_total), 0.0)
     )
     ineq = ebuf[...] == 1
 
@@ -294,10 +309,7 @@
     yn_s[...] = jnp.where(ineq, jnp.maximum(y_next, 0.0), y_next)
     p_resid = b - totals[:, LANES:]
     p_resid = jnp.where(ineq, jnp.maximum(p_resid, 0.0), p_resid)
-    primal_sum = jnp.sum(p_resid * p_resid, axis=0, keepdims=True)
-    sbuf[dev] = jnp.where(
-        sub8 == 0, primal_sum, jnp.where(sub8 == 1, dual_sum, jnp.where(sub8 == 2, gap, 0.0))
-    )
+    sbuf[dev] = jnp.where(lane1 == 0, total(p_resid * p_resid) / rows_total, early_stats)
 
     def s_copy(at, to, sem):
         return pltpu.make_async_remote_copy(
@@ -321,16 +333,14 @@
     yn_out.wait()
 
     each(n_dev, lambda k: s_copy(lax.rem(dev + k, n_dev), dev, k).wait_recv())
-    sums = jnp.sum(jnp.sum(sbuf[...], axis=0), axis=1, keepdims=True)
-    rows_total = ybuf.shape[1] * LANES * n_dev
-    cols_total = cblocks * LANES * n_dev
-    lane1 = iota((1, LANES), 1)
-    stat_o[...] = jnp.where(
-        lane1 == 0,
-        sums[0:1] / rows_total,
-        jnp.where(lane1 == 1, sums[1:2] / cols_total, sums[2:3] / math.sqrt(cols_total)),
-    )
+    stat_o[...] = jnp.sum(sbuf[...], axis=0)
     each(n_dev, lambda k: s_copy(dev, dev, k).wait_send())
+
+
+def hand_on(x_i, y_i, stat_i, x_o, y_o, stat_o):
+    x_o[...] = x_i[...]
+    y_o[...] = y_i[...]
+    stat_o[...] = stat_i[0, :3]
 
 
 def shards(
@@ -356,7 +366,6 @@
     rb = dual_iter.shape[1] // LANES
     wide = lambda a: a.reshape(-1, LANES)
     hbm = pl.BlockSpec(memory_space=pltpu.HBM)
-    smem = pl.BlockSpec(memory_space=pltpu.SMEM)
     vmem = pl.BlockSpec(memory_space=pltpu.VMEM)
     dma = pltpu.SemaphoreType.DMA
     x_next, y_next, stats = pl.pallas_call(
@@ -366,7 +375,7 @@
             jax.ShapeDtypeStruct((rb, LANES), F32),
             jax.ShapeDtypeStruct((1, LANES), F32),
         ),
-        in_specs=[hbm, smem, smem, smem, hbm, hbm, hbm, hbm, hbm, hbm, hbm, hbm, smem],
+        in_specs=[hbm] * 13,
         out_specs=(hbm, hbm, vmem),
         scratch_shapes=[
             pltpu.VMEM((count, size, size), BF16),
@@ -381,8 +390,12 @@
             pltpu.VMEM((rb, LANES), F32),
             pltpu.VMEM((n_col, rb, 2 * LANES), F32),
             pltpu.VMEM((n_col, rb, 2 * LANES), F32),
-            pltpu.VMEM((n_dev, 8, LANES), F32),
-            dma((14,)),
+            pltpu.VMEM((n_dev, 1, LANES), F32),
+            pltpu.SMEM((2, count), jnp.int32),
+            pltpu.SMEM(scale_index.shape, jnp.int32),
+            pltpu.SMEM(scale_table.shape, F32),
+            pltpu.SMEM(step_sizes.shape, F32),
+            dma((18,)),
             dma((n_col,)),
             dma((n_col,)),
             dma((7,)),
@@ -410,7 +423,19 @@
         wide(row_kind),
         step_sizes,
     )
-    return (x_next.reshape(1, -1), y_next.reshape(1, -1), stats[0, :3])
+    x_next, y_next, stats = pl.pallas_call(
+        hand_on,
+        out_shape=(
+            jax.ShapeDtypeStruct((cb, LANES), F32),
+            jax.ShapeDtypeStruct((rb, LANES), F32),
+            jax.ShapeDtypeStruct((3,), F32),
+        ),
+        in_specs=[vmem] * 3,
+        out_specs=(vmem, vmem, vmem),
+        scratch_shapes=[],
+        compiler_params=pltpu.CompilerParams(vmem_limit_bytes=64 * 1024 * 1024),
+    )(x_next, y_next, stats)
+    return (x_next.reshape(1, -1), y_next.reshape(1, -1), stats)
 
 
 def solution(mesh):

time: 27.1 us -> 23.7 us (0.87)
  local copies, waits for them, and re-layouts: 3.79 us -> 0 us
  Pallas kernels: 22.5 us -> 22.8 us
    unnamed x2 -> x0, local copies, waits for them, and re-layouts: 2.65 us -> none
    pallas_call x0 -> x1, Pallas kernels: none -> 1.39 us  [shards(): pl.pallas_call(hand_on, out_shape=(jax.ShapeDtypeStruct((cb, LANES), F32)...]
    squeeze x1 -> x0, local copies, waits for them, and re-layouts: 1.15 us -> none  [shards(): return (x_next.reshape(1, -1), y_next.reshape(1, -1), stats[0, :3])]
    pallas_call x1, Pallas kernels: 22.5 us -> 21.4 us  [shards(): pl.pallas_call(functools.partial(kernel, n_col, n_row), out_shape=(jax.Sh...]
where the time goes in v2:
time: 23.7 us; the launch traced here: 23.5 us
  Pallas kernels  22.8 us (96%)
  between operations  0.64 us (3%)
    pallas_call x1, Pallas kernels, shards(): pl.pallas_call(functools.partial(kernel, n_col, n_row), out_shape=(jax.Sh...  21.4 us
    pallas_call x1, Pallas kernels, shards(): pl.pallas_call(hand_on, out_shape=(jax.ShapeDtypeStruct((cb, LANES), F32)...  1.39 us

profile of v2, /device:TPU:0, one launch (start us, length us, event | category | flops | bytes accessed | tf_op | source)
XLA Modules:
  0.0 23.5 jit_solution(250216042943291587)
XLA Ops:
  0.6 21.4 %shard_map.148 = (f32[64,128]{1,0:T(8,128)}, f32[8,128]{1,0:T(8,128)}, f32[1,128]{1,0:T(1,128)}) custom-call(bf16[24,256,256]{2,1,0:T(8,128)(2,1)} %tv.1, s32[2,24]{1,0:T(2,128)} %bitcast.19, s32[24]{0:T(128)} %si_h.1, f32[16]{0:T(128)} %st_h.1, f32[64,128]{1,0:T(8,128)} %bitcast.11, f32[8,128]{1,0:T(8,128)} %bitcast.16, f32[64,128]{1,0:T(8,128)} %bitcast.12, ...), custom_call_target="tpu_custom_call" | custom-call | tf_op jit(solution)/shard_map/pallas_call | solution.py:371
  22.1 1.4 %shard_map.149 = (f32[64,128]{1,0:T(8,128)}, f32[8,128]{1,0:T(8,128)}, f32[3]{0:T(128)}) custom-call(f32[64,128]{1,0:T(8,128)} %get-tuple-element.9.x_i, f32[8,128]{1,0:T(8,128)} %get-tuple-element.10.y_i, f32[1,128]{1,0:T(1,128)} %get-tuple-element.11.stat_i), custom_call_target="tpu_custom_call" | custom-call | tf_op jit(solution)/shard_map/pallas_call | solution.py:426

commit v3 on v2

--- a/solution.py
+++ b/solution.py
@@ -30,6 +30,14 @@
     return hi, mid, low
 
 
+def far_first(me, count, k):
+    j = k - 1
+    up = lax.div(2 * me, count)
+    rising = j + lax.div(j + count - me, count)
+    falling = count - 1 - j - lax.div(j + 1 + me, count)
+    return up * rising + (1 - up) * falling
+
+
 def total(v):
     return jnp.sum(jnp.sum(v, axis=0, keepdims=True), axis=1, keepdims=True)
 
@@ -43,7 +51,7 @@
     n_row,
     tv, tb_h, si_h, st_h, x_h, y_h, c_h, b_h, l_h, u_h, k_h, e_h, step_h,
     xn_o, yn_o, stat_o,
-    tiles, prim, kind, ybuf, bbuf, ebuf, meta, part, xn_s, yn_s, terms, rt, sbuf,
+    tiles, flipped, prim, kind, ybuf, bbuf, ebuf, meta, part, xn_s, yn_s, terms, rt, sbuf,
     tb, si, st, step, lsem, ysend, yrecv, rsend, rrecv, tsend, trecv, ssend, srecv,
 ):
     count, size, _ = tv.shape
@@ -60,7 +68,7 @@
     barrier = pltpu.get_barrier_semaphore()
 
     def greet(k):
-        q = lax.rem(dev + k, n_dev)
+        q = far_first(dev, n_dev, k)
         pl.semaphore_signal(
             barrier,
             inc=1,
@@ -124,7 +132,7 @@
             device_id_type=MESH,
         )
 
-    each(n_col, lambda k: y_copy(col, lax.rem(col + k, n_col), k).start())
+    each(n_col, lambda k: y_copy(col, far_first(col, n_col, k), k).start())
 
     def row_copy(src, dst, i):
         return pltpu.make_async_remote_copy(
@@ -183,6 +191,8 @@
 
     for copy in tile_in:
         copy.wait()
+    for s in range(count):
+        flipped[s * size : (s + 1) * size] = tiles[s].T
     each(n_col, lambda k: y_copy(lax.rem(col + k, n_col), col, k).wait_recv())
 
     y_b = ybuf[...].reshape(wide_rows, LANES).astype(BF16)
@@ -230,20 +240,17 @@
     p_pick = jnp.concatenate(
         [jnp.dot(pick, pair, preferred_element_type=F32) for pick in pick_p], axis=1
     )
-    sub16 = iota((16, size), 0) % 8
-    bars, news = [], []
-    for g in range(groups):
-        rows16 = p_pick[16 * g : 16 * g + 16]
-        acc = jnp.zeros((16, size), F32)
-        for t in range(8):
-            acc = acc + lax.dot_general(
-                jnp.where(sub16 == t, rows16, 0.0).astype(BF16),
-                tiles[8 * g + t],
-                (((1,), (1,)), ((), ())),
-                preferred_element_type=F32,
-            )
-        bars.append(acc[:8] * scale8[g])
-        news.append(acc[8:] * scale8[g])
+    sub_p = iota(p_pick.shape, 0)
+    lhs = jnp.concatenate(
+        [
+            jnp.where((sub_p % 8 == s % 8) & (sub_p // 16 == s // 8), p_pick, 0.0).astype(BF16)
+            for s in range(count)
+        ],
+        axis=1,
+    )
+    acc = jnp.dot(lhs, flipped[...], preferred_element_type=F32)
+    bars = [acc[16 * g : 16 * g + 8] * scale8[g] for g in range(groups)]
+    news = [acc[16 * g + 8 : 16 * g + 16] * scale8[g] for g in range(groups)]
     bar = jnp.concatenate(bars, axis=0)
     new = jnp.concatenate(news, axis=0)
     stacked = jnp.concatenate(
@@ -268,7 +275,7 @@
         )
 
     def t_start(k):
-        to = lax.rem(col + k, n_col)
+        to = far_first(col, n_col, k)
         t_copy(to, col, to, k).start()
 
     each(n_col, t_start)
@@ -309,19 +316,21 @@
     yn_s[...] = jnp.where(ineq, jnp.maximum(y_next, 0.0), y_next)
     p_resid = b - totals[:, LANES:]
     p_resid = jnp.where(ineq, jnp.maximum(p_resid, 0.0), p_resid)
-    sbuf[dev] = jnp.where(lane1 == 0, total(p_resid * p_resid) / rows_total, early_stats)
+    sbuf[0] = jnp.where(lane1 == 0, total(p_resid * p_resid) / rows_total, early_stats)
 
     def s_copy(at, to, sem):
         return pltpu.make_async_remote_copy(
-            src_ref=sbuf.at[dev],
-            dst_ref=sbuf.at[at],
+            src_ref=sbuf.at[0],
+            dst_ref=stat_o.at[at],
             send_sem=ssend.at[sem],
             recv_sem=srecv.at[at],
             device_id={"col": lax.div(to, n_row), "row": lax.rem(to, n_row)},
             device_id_type=MESH,
         )
 
-    each(n_dev, lambda k: s_copy(dev, lax.rem(dev + k, n_dev), k).start())
+    each(n_dev, lambda k: s_copy(dev, far_first(dev, n_dev, k), k).start())
+    own_stat = pltpu.make_async_copy(sbuf.at[0], stat_o.at[dev], lsem.at[18])
+    own_stat.start()
     yn_out = pltpu.make_async_copy(yn_s, yn_o, lsem.at[13])
     yn_out.start()
     for copy in early:
@@ -333,14 +342,14 @@
     yn_out.wait()
 
     each(n_dev, lambda k: s_copy(lax.rem(dev + k, n_dev), dev, k).wait_recv())
-    stat_o[...] = jnp.sum(sbuf[...], axis=0)
+    own_stat.wait()
     each(n_dev, lambda k: s_copy(dev, dev, k).wait_send())
 
 
 def hand_on(x_i, y_i, stat_i, x_o, y_o, stat_o):
     x_o[...] = x_i[...]
     y_o[...] = y_i[...]
-    stat_o[...] = stat_i[0, :3]
+    stat_o[...] = jnp.sum(stat_i[...], axis=0)[0, :3]
 
 
 def shards(
@@ -373,12 +382,13 @@
         out_shape=(
             jax.ShapeDtypeStruct((cb, LANES), F32),
             jax.ShapeDtypeStruct((rb, LANES), F32),
-            jax.ShapeDtypeStruct((1, LANES), F32),
+            jax.ShapeDtypeStruct((n_dev, 1, LANES), F32),
         ),
         in_specs=[hbm] * 13,
-        out_specs=(hbm, hbm, vmem),
+        out_specs=(hbm, hbm, hbm),
         scratch_shapes=[
             pltpu.VMEM((count, size, size), BF16),
+            pltpu.VMEM((count * size, size), BF16),
             pltpu.VMEM((4, n_row, cb, LANES), F32),
             pltpu.VMEM((n_row, cb, LANES), jnp.int32),
             pltpu.VMEM((n_col, rb, LANES), F32),
@@ -390,12 +400,12 @@
             pltpu.VMEM((rb, LANES), F32),
             pltpu.VMEM((n_col, rb, 2 * LANES), F32),
             pltpu.VMEM((n_col, rb, 2 * LANES), F32),
-            pltpu.VMEM((n_dev, 1, LANES), F32),
+            pltpu.VMEM((1, 1, LANES), F32),
             pltpu.SMEM((2, count), jnp.int32),
             pltpu.SMEM(scale_index.shape, jnp.int32),
             pltpu.SMEM(scale_table.shape, F32),
             pltpu.SMEM(step_sizes.shape, F32),
-            dma((18,)),
+            dma((19,)),
             dma((n_col,)),
             dma((n_col,)),
             dma((7,)),

time: 23.7 us -> 22.8 us (0.962)
  Pallas kernels: 22.8 us -> 22 us
    pallas_call x1, Pallas kernels: 21.4 us -> 20.6 us  [shards(): pl.pallas_call(functools.partial(kernel, n_col, n_row), out_shape=(jax.Sh...]
where the time goes in v3:
time: 22.8 us; the launch traced here: 22.6 us
  Pallas kernels  22 us (96%)
  between operations  0.64 us (3%)
    pallas_call x1, Pallas kernels, shards(): pl.pallas_call(functools.partial(kernel, n_col, n_row), out_shape=(jax.Sh...  20.6 us
    pallas_call x1, Pallas kernels, shards(): pl.pallas_call(hand_on, out_shape=(jax.ShapeDtypeStruct((cb, LANES), F32)...  1.39 us

profile of v3, /device:TPU:0, one launch (start us, length us, event | category | flops | bytes accessed | tf_op | source)
XLA Modules:
  0.0 22.6 jit_solution(9913917756113793057)
XLA Ops:
  0.6 20.6 %shard_map.148 = (f32[64,128]{1,0:T(8,128)}, f32[8,128]{1,0:T(8,128)}, f32[16,1,128]{2,1,0:T(1,128)}) custom-call(bf16[24,256,256]{2,1,0:T(8,128)(2,1)} %tv.1, s32[2,24]{1,0:T(2,128)} %bitcast.19, s32[24]{0:T(128)} %si_h.1, f32[16]{0:T(128)} %st_h.1, f32[64,128]{1,0:T(8,128)} %bitcast.11, f32[8,128]{1,0:T(8,128)} %bitcast.16, f32[64,128]{1,0:T(8,128)} %bitcast.12, ...), custom_call_target="tpu_custom_call" | custom-call | tf_op jit(solution)/shard_map/pallas_call | solution.py:380
  21.2 1.4 %shard_map.149 = (f32[64,128]{1,0:T(8,128)}, f32[8,128]{1,0:T(8,128)}, f32[3]{0:T(128)}) custom-call(f32[64,128]{1,0:T(8,128)} %get-tuple-element.9.x_i, f32[8,128]{1,0:T(8,128)} %get-tuple-element.10.y_i, f32[16,1,128]{2,1,0:T(1,128)} %get-tuple-element.11.stat_i), custom_call_target="tpu_custom_call" | custom-call | tf_op jit(solution)/shard_map/pallas_call | solution.py:436

commit v4 on v3

--- a/solution.py
+++ b/solution.py
@@ -199,12 +199,16 @@
     y_pick = jnp.concatenate(
         [jnp.dot(pick, y_b, preferred_element_type=F32) for pick in pick_y], axis=1
     )
-    sub_y = iota(y_pick.shape, 0)
-    lhs = jnp.concatenate(
-        [jnp.where(sub_y == s, y_pick, 0.0).astype(BF16) for s in range(count)], axis=1
-    )
-    product = jnp.dot(lhs, tiles[...].reshape(count * size, size), preferred_element_type=F32)
-    product = product * jnp.concatenate(scale8 + [jnp.zeros((8, 2 * LANES), F32)], axis=0)
+    sub_y = iota((8, size), 0)
+    product = []
+    for g in range(groups):
+        rows8 = y_pick[8 * g : 8 * g + 8]
+        lhs = jnp.concatenate(
+            [jnp.where(sub_y == t, rows8, 0.0) for t in range(8)], axis=1
+        ).astype(BF16)
+        weights = tiles[8 * g : 8 * g + 8].reshape(8 * size, size)
+        product.append(jnp.dot(lhs, weights, preferred_element_type=F32) * scale8[g])
+    product = jnp.concatenate(product + [jnp.zeros((8, size), F32)], axis=0)
     part[row, 0] = product[:, :LANES]
     part[row, 1] = product[:, LANES:]
     part_copy = row_copy(part.at[row], part.at[row], 6)
@@ -240,17 +244,17 @@
     p_pick = jnp.concatenate(
         [jnp.dot(pick, pair, preferred_element_type=F32) for pick in pick_p], axis=1
     )
-    sub_p = iota(p_pick.shape, 0)
-    lhs = jnp.concatenate(
-        [
-            jnp.where((sub_p % 8 == s % 8) & (sub_p // 16 == s // 8), p_pick, 0.0).astype(BF16)
-            for s in range(count)
-        ],
-        axis=1,
-    )
-    acc = jnp.dot(lhs, flipped[...], preferred_element_type=F32)
-    bars = [acc[16 * g : 16 * g + 8] * scale8[g] for g in range(groups)]
-    news = [acc[16 * g + 8 : 16 * g + 16] * scale8[g] for g in range(groups)]
+    sub_p = iota((16, size), 0) % 8
+    bars, news = [], []
+    for g in range(groups):
+        rows16 = p_pick[16 * g : 16 * g + 16]
+        lhs = jnp.concatenate(
+            [jnp.where(sub_p == t, rows16, 0.0).astype(BF16) for t in range(8)], axis=1
+        )
+        weights = flipped[8 * g * size : 8 * (g + 1) * size]
+        acc = jnp.dot(lhs, weights, preferred_element_type=F32)
+        bars.append(acc[:8] * scale8[g])
+        news.append(acc[8:] * scale8[g])
     bar = jnp.concatenate(bars, axis=0)
     new = jnp.concatenate(news, axis=0)
     stacked = jnp.concatenate(

time: 22.8 us -> 22.3 us (0.978)
  Pallas kernels: 22 us -> 21.4 us
    pallas_call x1, Pallas kernels: 20.6 us -> 20.1 us  [shards(): pl.pallas_call(functools.partial(kernel, n_col, n_row), out_shape=(jax.Sh...]
where the time goes in v4:
time: 22.3 us; the launch traced here: 22.1 us
  Pallas kernels  21.4 us (96%)
  between operations  0.64 us (3%)
    pallas_call x1, Pallas kernels, shards(): pl.pallas_call(functools.partial(kernel, n_col, n_row), out_shape=(jax.Sh...  20.1 us
    pallas_call x1, Pallas kernels, shards(): pl.pallas_call(hand_on, out_shape=(jax.ShapeDtypeStruct((cb, LANES), F32)...  1.39 us

profile of v4, /device:TPU:0, one launch (start us, length us, event | category | flops | bytes accessed | tf_op | source)
XLA Modules:
  0.0 22.1 jit_solution(14978755864289287562)
XLA Ops:
  0.6 20.1 %shard_map.148 = (f32[64,128]{1,0:T(8,128)}, f32[8,128]{1,0:T(8,128)}, f32[16,1,128]{2,1,0:T(1,128)}) custom-call(bf16[24,256,256]{2,1,0:T(8,128)(2,1)} %tv.1, s32[2,24]{1,0:T(2,128)} %bitcast.19, s32[24]{0:T(128)} %si_h.1, f32[16]{0:T(128)} %st_h.1, f32[64,128]{1,0:T(8,128)} %bitcast.11, f32[8,128]{1,0:T(8,128)} %bitcast.16, f32[64,128]{1,0:T(8,128)} %bitcast.12, ...), custom_call_target="tpu_custom_call" | custom-call | tf_op jit(solution)/shard_map/pallas_call | solution.py:384
  20.7 1.4 %shard_map.149 = (f32[64,128]{1,0:T(8,128)}, f32[8,128]{1,0:T(8,128)}, f32[3]{0:T(128)}) custom-call(f32[64,128]{1,0:T(8,128)} %get-tuple-element.9.x_i, f32[8,128]{1,0:T(8,128)} %get-tuple-element.10.y_i, f32[16,1,128]{2,1,0:T(1,128)} %get-tuple-element.11.stat_i), custom_call_target="tpu_custom_call" | custom-call | tf_op jit(solution)/shard_map/pallas_call | solution.py:440

commit v5 on v4

--- a/solution.py
+++ b/solution.py
@@ -189,10 +189,10 @@
         tgt_r = jnp.where(live & (spot3 == count + s), 2 * rows_l[s] + 1, tgt_r)
     place_r = (iota((wide_rows, 2 * LANES), 0) == tgt_r[0:1]).astype(F32).astype(BF16)
 
-    for copy in tile_in:
+    for i, copy in enumerate(tile_in):
         copy.wait()
-    for s in range(count):
-        flipped[s * size : (s + 1) * size] = tiles[s].T
+        for s in range(i * chunk, (i + 1) * chunk):
+            flipped[s * size : (s + 1) * size] = tiles[s].T
     each(n_col, lambda k: y_copy(lax.rem(col + k, n_col), col, k).wait_recv())
 
     y_b = ybuf[...].reshape(wide_rows, LANES).astype(BF16)
@@ -337,16 +337,16 @@
     own_stat.start()
     yn_out = pltpu.make_async_copy(yn_s, yn_o, lsem.at[13])
     yn_out.start()
+    xn_out.wait()
+    yn_out.wait()
+
+    each(n_dev, lambda k: s_copy(lax.rem(dev + k, n_dev), dev, k).wait_recv())
+    own_stat.wait()
     for copy in early:
         copy.wait_send()
     part_copy.wait_send()
     each(n_col, lambda k: y_copy(col, col, k).wait_send())
     each(n_col, lambda k: t_copy(0, col, col, k).wait_send())
-    xn_out.wait()
-    yn_out.wait()
-
-    each(n_dev, lambda k: s_copy(lax.rem(dev + k, n_dev), dev, k).wait_recv())
-    own_stat.wait()
     each(n_dev, lambda k: s_copy(dev, dev, k).wait_send())
 
 

time: 22.3 us -> 22.3 us (level)
  no operation moved by 1% of the time
where the time goes in v5:
time: 22.3 us; the launch traced here: 22.1 us
  Pallas kernels  21.5 us (96%)
  between operations  0.64 us (3%)
    pallas_call x1, Pallas kernels, shards(): pl.pallas_call(functools.partial(kernel, n_col, n_row), out_shape=(jax.Sh...  20.1 us
    pallas_call x1, Pallas kernels, shards(): pl.pallas_call(hand_on, out_shape=(jax.ShapeDtypeStruct((cb, LANES), F32)...  1.39 us

profile of v5, /device:TPU:0, one launch (start us, length us, event | category | flops | bytes accessed | tf_op | source)
XLA Modules:
  0.0 22.1 jit_solution(17733850742115126808)
XLA Ops:
  0.6 20.1 %shard_map.148 = (f32[64,128]{1,0:T(8,128)}, f32[8,128]{1,0:T(8,128)}, f32[16,1,128]{2,1,0:T(1,128)}) custom-call(bf16[24,256,256]{2,1,0:T(8,128)(2,1)} %tv.1, s32[2,24]{1,0:T(2,128)} %bitcast.19, s32[24]{0:T(128)} %si_h.1, f32[16]{0:T(128)} %st_h.1, f32[64,128]{1,0:T(8,128)} %bitcast.11, f32[8,128]{1,0:T(8,128)} %bitcast.16, f32[64,128]{1,0:T(8,128)} %bitcast.12, ...), custom_call_target="tpu_custom_call" | custom-call | tf_op jit(solution)/shard_map/pallas_call | solution.py:384
  20.7 1.4 %shard_map.149 = (f32[64,128]{1,0:T(8,128)}, f32[8,128]{1,0:T(8,128)}, f32[3]{0:T(128)}) custom-call(f32[64,128]{1,0:T(8,128)} %get-tuple-element.9.x_i, f32[8,128]{1,0:T(8,128)} %get-tuple-element.10.y_i, f32[16,1,128]{2,1,0:T(1,128)} %get-tuple-element.11.stat_i), custom_call_target="tpu_custom_call" | custom-call | tf_op jit(solution)/shard_map/pallas_call | solution.py:440
